TPU v7x, 32 devices: a whole 2x2x4 slice. The times are simulated.
32 devices in a mesh: obs: 4 (over y, x), par: 8 (over z, core).
Axes of the slice: x: 2, y: 2, z: 4, core: 2. Of those that a mesh axis runs over, the one named last changes fastest.
Arguments:
- design: bfloat16 [1024, 12288], P('obs', 'par'), may hold values from -3 to 3
- filter_taps: float32 [2, 512], replicated, may hold values from -0.4 to 5
- band_limit: int32 [2], replicated, may hold values from 128 to 512, as said below
- col_order: int32 [8], replicated, may hold values from 0 to 7, each once
Outputs:
- normal: float32 [12288, 12288], P('par', 'obs')
Inputs may be any that keep to these rules, and one draw needn't show every extreme that they name: col_order names every parameter block once. `band_limit`: the first arc batch uses all 512 lags.
All inputs are finite; a program needn't handle non-finite values.
Results may differ from a plain program's by a relative error of at most 0.0051.
Values may be sent and summed in bfloat16 or wider, within the bound.
A program may use at most 128 MiB of HBM per device.

v0:
```python
import functools

import jax
import jax.numpy as jnp
from jax import lax
from jax.experimental import pallas as pl
from jax.experimental.pallas import tpu as pltpu
from jax.sharding import PartitionSpec as P

MESH = pl.DeviceIdType.MESH
LANES = 128


def build_filters(taps_ref, limit_ref, filt_ref):
    arcs, arc_len = taps_ref.shape
    tiles = arc_len // LANES
    row = lax.broadcasted_iota(jnp.int32, (LANES, 2 * LANES), 0)
    upper = lax.broadcasted_iota(jnp.int32, (LANES, LANES), 1) >= lax.broadcasted_iota(
        jnp.int32, (LANES, LANES), 0
    )
    lag = lax.broadcasted_iota(jnp.int32, (1, arc_len), 1)
    for a in range(arcs):
        taps = taps_ref[a : a + 1, :].astype(jnp.bfloat16).astype(jnp.float32)
        taps = jnp.where(lag < limit_ref[a], taps, 0.0)
        for d in range(tiles):
            before = taps[:, (d - 1) * LANES : d * LANES] if d else jnp.zeros((1, LANES), jnp.float32)
            strip = jnp.concatenate([before, taps[:, d * LANES : (d + 1) * LANES]], axis=1)
            strip = jnp.broadcast_to(strip, (LANES, 2 * LANES))
            step = 1
            while step < LANES:
                strip = jnp.where((row & step) != 0, pltpu.roll(strip, step, 1), strip)
                step *= 2
            tile = strip[:, LANES:]
            mirrored = tile.T
            if d == 0:
                tile = jnp.where(upper, tile, mirrored)
            tile_low, mirrored_low = tile.astype(jnp.bfloat16), mirrored.astype(jnp.bfloat16)
            for i in range(tiles - d):
                lo, hi = pl.ds(i * LANES, LANES), pl.ds((i + d) * LANES, LANES)
                filt_ref[a, lo, hi] = tile_low
                if d:
                    filt_ref[a, hi, lo] = mirrored_low


def gather_kernel(
    obs_size, par_size, width, early,
    design_ref, taps_ref, limit_ref, order_ref,
    own_ref, part_ref, early_ref,
    raw_ref, filt_ref, stage_ref, mixed_ref,
    place_sem, across_s, across_r, line_s, line_r,
    own_s, own_r, swap_s, swap_r, back_s, back_r,
    *pools,
):
    arcs, arc_len, columns = raw_ref.shape
    rows = design_ref.shape[0]
    epochs = rows // arcs
    chunks = columns // (2 * width)
    total = arcs * arc_len
    blocks_per = par_size // obs_size
    chips = par_size // 2
    hops = chips - 1
    o, p = lax.axis_index("obs"), lax.axis_index("par")
    k, core = p // 2, p % 2
    other = k * 2 + 1 - core

    def obs_peer(d):
        return lax.rem(o + d, obs_size)

    def obs_source(d):
        return lax.rem(o + obs_size - d, obs_size)

    def device(obs, par):
        return {"obs": obs, "par": par}

    def epochs_of(obs):
        return pl.ds(pl.multiple_of(obs * epochs, epochs), epochs)

    def lanes_of(which, g=0):
        return pl.ds(pl.multiple_of((2 * g + which) * width, LANES), width)

    barrier = pltpu.get_barrier_semaphore()
    for d in range(1, obs_size):
        pl.semaphore_signal(barrier, inc=1, device_id=device(obs_peer(d), p), device_id_type=MESH)
    pl.semaphore_signal(barrier, inc=1, device_id=device(o, other), device_id_type=MESH)

    @pl.when(k < hops)
    def _():
        pl.semaphore_signal(barrier, inc=1, device_id=device(o, p + 2), device_id_type=MESH)

    @pl.when(k > 0)
    def _():
        pl.semaphore_signal(barrier, inc=1, device_id=device(o, p - 2), device_id_type=MESH)

    target = lax.broadcasted_iota(jnp.int32, (rows, rows), 0)
    source = lax.broadcasted_iota(jnp.int32, (rows, rows), 1)
    wanted = target * arcs
    for a in range(1, arcs):
        wanted = jnp.where(target >= a * epochs, (target - a * epochs) * arcs + a, wanted)
    sort = jnp.where(source == wanted, 1.0, 0.0).astype(jnp.bfloat16)
    for lo in range(0, columns, 512):
        size = min(512, columns - lo)
        tile = jnp.dot(sort, design_ref[:, lo : lo + size], preferred_element_type=jnp.float32)
        tile = tile.astype(jnp.bfloat16)
        for a in range(arcs):
            raw_ref[a, epochs_of(o), lo : lo + size] = tile[a * epochs : (a + 1) * epochs]

    near = jnp.where(k < hops, 1, 0) + jnp.where(k > 0, 1, 0)
    pl.semaphore_wait(barrier, obs_size + near)

    sent = []

    def place(g):
        return pltpu.make_async_copy(
            raw_ref.at[:, epochs_of(o), lanes_of(core, g)], pools[g].at[p], place_sem.at[g]
        )

    def across(g):
        return pltpu.make_async_remote_copy(
            raw_ref.at[:, epochs_of(o), lanes_of(1 - core, g)], pools[g].at[p],
            across_s.at[g], across_r.at[g], device_id=device(o, other), device_id_type=MESH,
        )

    def across_in(g):
        return pltpu.make_async_remote_copy(
            pools[g].at[other], pools[g].at[other],
            across_s.at[g], across_r.at[g], device_id=device(o, other), device_id_type=MESH,
        )

    def line(g, way, s, incoming):
        if way == 0:
            pair, to = (k - 1 - s if incoming else k - s), p + 2
        else:
            pair, to = (k + 1 + s if incoming else k + s), p - 2
        window = pools[g].at[pl.ds(pair * 2, 2)]
        return pltpu.make_async_remote_copy(
            window, window, line_s.at[way, g, s], line_r.at[way, g, s],
            device_id=device(o, to), device_id_type=MESH,
        )

    def ahead(s):
        return 2 if s == 0 else 1

    def sends(way, s):
        return ((k >= s) & (k < hops)) if way == 0 else ((k + s < chips) & (k > 0))

    def receives(way, s):
        return (k - 1 - s >= 0) if way == 0 else (k + 1 + s < chips)

    def line_wait(g, s):
        for way in (0, 1):
            @pl.when(receives(way, s))
            def _():
                line(g, way, s, True).wait_recv()

    def line_send(g, s):
        for way in (0, 1):
            @pl.when(sends(way, s))
            def _():
                if g >= ahead(s):
                    line(g - ahead(s), way, s, False).wait_send()
                line(g, way, s, False).start()

    square = obs_size == 4 and arcs == 2
    first = lax.rem(o, 2)
    beside = (o - first + 1 - first, 2 - o + 2 * first)

    def own_copy(d, owner):
        window = raw_ref.at[:, epochs_of(owner), :]
        return pltpu.make_async_remote_copy(
            window, window, own_s.at[d - 1], own_r.at[d - 1],
            device_id=device(obs_peer(d), p), device_id_type=MESH,
        )

    def own_arc(way, a, owner, slot):
        window = raw_ref.at[a, epochs_of(owner), :]
        return pltpu.make_async_remote_copy(
            window, window, own_s.at[slot], own_r.at[slot],
            device_id=device(beside[way], p), device_id_type=MESH,
        )

    def own_send(a):
        if square:
            for way in range(2):
                copy = own_arc(way, (a + way) % 2, o, 3 * way + a)
                copy.start()
                sent.append(copy)
        elif a == 0:
            for d in range(1, obs_size):
                own_copy(d, o).start()
                sent.append(own_copy(d, o))

    def own_forward():
        if square:
            for way in range(2):
                own_arc(way, way, beside[way], 3 * way).wait_recv()
            for way in range(2):
                copy = own_arc(1 - way, way, beside[way], 3 * (1 - way) + 2)
                copy.start()
                sent.append(copy)

    def own_wait():
        if square:
            for way in range(2):
                own_arc(way, 1 - way, beside[way], 3 * way + 1).wait_recv()
                own_arc(way, 1 - way, 3 - o, 3 * way + 2).wait_recv()
        else:
            for d in range(1, obs_size):
                own_copy(d, obs_source(d)).wait_recv()

    def swap(g, d, owner):
        return pltpu.make_async_remote_copy(
            stage_ref.at[g, d - 1], mixed_ref.at[g, :, epochs_of(owner), :],
            swap_s.at[g, d - 1], swap_r.at[g, d - 1],
            device_id=device(obs_peer(d), p), device_id_type=MESH,
        )

    def back(g, which):
        window = part_ref.at[g, :, :, lanes_of(which)]
        return pltpu.make_async_remote_copy(
            window, window, back_s.at[g], back_r.at[g],
            device_id=device(o, other), device_id_type=MESH,
        )

    def filter_own(begin, end):
        size = 2 * width

        @pl.loop(begin, end)
        def _(i):
            lanes = pl.ds(pl.multiple_of(i * size, size), size)
            for a in range(arcs):
                value = jnp.dot(filt_ref[a], raw_ref[a, :, lanes], preferred_element_type=jnp.float32)
                own_ref[lanes, a * arc_len : (a + 1) * arc_len] = value.T.astype(jnp.bfloat16)

    def filter_chunk(g):
        for d in range(1, obs_size):
            swap(g, d, obs_source(d)).wait_recv()
        for a in range(arcs):
            value = jnp.dot(filt_ref[a], mixed_ref[g, a], preferred_element_type=jnp.float32)
            value = value.astype(jnp.bfloat16)
            for j in range(blocks_per):
                part_ref[g, j, a * arc_len : (a + 1) * arc_len, lanes_of(core)] = (
                    value[:, j * width : (j + 1) * width]
                )
        back(g, core).start()
        sent.append(back(g, core))

    def early_product(g):
        back(g, 1 - core).wait_recv()
        for j in range(blocks_per):
            @pl.loop(0, columns // 256)
            def _(i):
                here = pl.ds(pl.multiple_of(i * 256, 256), 256)
                value = jnp.dot(own_ref[here, :], part_ref[g, j], preferred_element_type=jnp.float32)
                early_ref[j, here, g * 256 : (g + 1) * 256] = value * (1.0 / total)

    for g in range(chunks):
        place(g).start()
        across(g).start()
        sent.append(across(g))

    def first_send(g):
        place(g).wait()
        across_in(g).wait_recv()
        line_send(g, 0)

    own_send(0)
    for g in range(min(2, chunks)):
        first_send(g)
    build_filters(taps_ref, limit_ref, filt_ref)

    done = 0
    for stage in range(1, chunks + hops):
        for s in range(1, hops):
            g = stage - s
            if 0 <= g < chunks:
                line_wait(g, s - 1)
                line_send(g, s)
        if stage + 1 < chunks:
            first_send(stage + 1)
        if stage == 1:
            own_send(1)
        g = stage - hops
        if 0 <= g < chunks:
            line_wait(g, hops - 1)
            if g == 0:
                own_forward()
            for d in range(1, obs_size):
                for j in range(blocks_per):
                    block = order_ref[obs_peer(d) * blocks_per + j]
                    stage_ref[g, d - 1, :, :, j * width : (j + 1) * width] = pools[g][block]
                swap(g, d, o).start()
                sent.append(swap(g, d, o))
            for j in range(blocks_per):
                block = order_ref[o * blocks_per + j]
                mixed_ref[g, :, epochs_of(o), j * width : (j + 1) * width] = pools[g][block]

        left = chunks + hops - 1 - stage
        if left < 3:
            if left == 2:
                own_wait()
            else:
                filter_chunk(done)
                done += 1
            filter_own(chunks * (2 - left) // 3, chunks * (3 - left) // 3)

    made = 0
    for g in range(done, chunks):
        filter_chunk(g)
        if made < early and g < chunks - 1:
            early_product(made)
            made += 1
    for g in range(made, early):
        early_product(g)
    for g in range(early, chunks):
        back(g, 1 - core).wait_recv()
    for copy in sent:
        copy.wait_send()
    for s in range(hops):
        for g in range(max(chunks - ahead(s), 0), chunks):
            for way in (0, 1):
                @pl.when(sends(way, s))
                def _():
                    line(g, way, s, False).wait_send()


def product_kernel(early, own_ref, part_ref, early_ref, out_ref, late_ref, early_s, late_s):
    columns, total = own_ref.shape
    chunks, blocks_per, _, size = part_ref.shape
    split = early * size
    rest = columns - split
    bands = late_s.shape[0]
    rows = columns // bands

    def early_copy(j):
        lanes = pl.ds(j * columns, split)
        return pltpu.make_async_copy(early_ref.at[j], out_ref.at[:, lanes], early_s.at[j])

    def late_copy(i, j):
        here = pl.ds(pl.multiple_of(i * rows, rows), rows)
        lanes = pl.ds(j * columns + split, rest)
        return pltpu.make_async_copy(late_ref.at[j, here, :], out_ref.at[here, lanes], late_s.at[i, j])

    for j in range(blocks_per):
        early_copy(j).start()

    @pl.loop(0, bands)
    def _(i):
        here = pl.ds(pl.multiple_of(i * rows, rows), rows)
        for j in range(blocks_per):
            for g in range(early, chunks):
                value = jnp.dot(own_ref[here, :], part_ref[g, j], preferred_element_type=jnp.float32)
                lo = (g - early) * size
                late_ref[j, here, lo : lo + size] = value * (1.0 / total)
            late_copy(i, j).start()

    for i in range(bands):
        for j in range(blocks_per):
            late_copy(i, j).wait()
    for j in range(blocks_per):
        early_copy(j).wait()


def per_device(obs_size, par_size, design, filter_taps, band_limit, col_order):
    rows, columns = design.shape
    arcs, arc_len = filter_taps.shape
    epochs = rows // arcs
    total = arcs * arc_len
    blocks_per = par_size // obs_size
    width = LANES
    size = 2 * width
    chunks = columns // size
    hops = par_size // 2 - 1
    early = chunks // 2
    split = early * size
    bands = 3
    low, full = jnp.bfloat16, jnp.float32
    vmem, smem = pl.BlockSpec(memory_space=pltpu.VMEM), pl.BlockSpec(memory_space=pltpu.SMEM)
    anywhere = pl.BlockSpec(memory_space=pl.ANY)
    dma = pltpu.SemaphoreType.DMA
    own, part, made = pl.pallas_call(
        functools.partial(gather_kernel, obs_size, par_size, width, early),
        out_shape=(
            pltpu.VMEM((columns, total), low),
            pltpu.VMEM((chunks, blocks_per, total, size), low),
            pltpu.VMEM((blocks_per, columns, split), full),
        ),
        in_specs=[vmem, vmem, smem, smem],
        out_specs=(vmem, vmem, vmem),
        scratch_shapes=[
            pltpu.VMEM((arcs, arc_len, columns), low),
            pltpu.VMEM((arcs, arc_len, arc_len), low),
            pltpu.VMEM((chunks, obs_size - 1, arcs, epochs, blocks_per * width), low),
            pltpu.VMEM((chunks, arcs, arc_len, blocks_per * width), low),
            dma((chunks,)), dma((chunks,)), dma((chunks,)),
            dma((2, chunks, hops)), dma((2, chunks, hops)),
            dma((max(6, obs_size),)), dma((max(6, obs_size),)),
            dma((chunks, obs_size - 1)), dma((chunks, obs_size - 1)),
            dma((chunks,)), dma((chunks,)),
        ]
        + [pltpu.VMEM((par_size, arcs, epochs, width), low) for _ in range(chunks)],
        compiler_params=pltpu.CompilerParams(
            collective_id=0, has_side_effects=True, vmem_limit_bytes=36 * 1024 * 1024
        ),
    )(design, filter_taps, band_limit, col_order)
    return pl.pallas_call(
        functools.partial(product_kernel, early),
        out_shape=jax.ShapeDtypeStruct((columns, blocks_per * columns), full),
        in_specs=[vmem, vmem, vmem],
        out_specs=anywhere,
        scratch_shapes=[
            pltpu.VMEM((blocks_per, columns, columns - split), full),
            dma((blocks_per,)), dma((bands, blocks_per)),
        ],
        compiler_params=pltpu.CompilerParams(vmem_limit_bytes=24 * 1024 * 1024),
    )(own, part, made)


def solution(mesh):
    body = functools.partial(per_device, mesh.shape["obs"], mesh.shape["par"])
    placed = (P("obs", "par"), P(), P(), P())
    return jax.shard_map(body, mesh=mesh, in_specs=placed, out_specs=P("par", "obs"), check_vma=False)
```

profile of v0, /device:TPU:0, one launch (start us, length us, event | category | flops | bytes accessed | tf_op | source)
XLA Modules:
  0.0 83.7 jit_solution(12105122566541274586)
XLA Ops:
  0.0 76.9 %shard_map.46 = (bf16[1536,1024]{1,0:T(8,128)(2,1)S(1)}, bf16[6,2,1024,256]{3,2,1,0:T(8,128)(2,1)S(1)}, f32[2,1536,768]{2,1,0:T(8,128)S(1)}) custom-call(bf16[256,1536]{1,0:T(8,128)(2,1)} %design_ref.1, f32[2,512]{1,0:T(2,128)} %taps_ref.1, s32[2]{0:T(128)} %limit_ref.1, s32[8]{0:T(128)} %order_ref.1), custom_call_target="tpu_custom_call" | custom-call | tf_op jit(solution)/shard_map/pallas_call | solution.py:380
  76.9 6.7 %shard_map.47 = f32[1536,3072]{1,0:T(8,128)} custom-call(bf16[1536,1024]{1,0:T(8,128)(2,1)S(1)} %get-tuple-element.8.own_ref, bf16[6,2,1024,256]{3,2,1,0:T(8,128)(2,1)S(1)} %get-tuple-element.9.part_ref, f32[2,1536,768]{2,1,0:T(8,128)S(1)} %get-tuple-element.10.early_ref), custom_call_target="tpu_custom_call" | custom-call | tf_op jit(solution)/shard_map/pallas_call | solution.py:405
where the time goes:
time: 83.8 us; the launch traced here: 83.7 us
  Pallas kernels  83.7 us (100%)
    pallas_call x1, Pallas kernels, per_device(): pl.pallas_call(functools.partial(gather_kernel, obs_size, par_size, width...  76.9 us
    pallas_call x1, Pallas kernels, per_device(): pl.pallas_call(functools.partial(product_kernel, early), out_shape=jax.Sh...  6.74 us

commit v1 on v0

--- a/solution.py
+++ b/solution.py
@@ -137,9 +137,6 @@
             device_id=device(o, to), device_id_type=MESH,
         )
 
-    def ahead(s):
-        return 2 if s == 0 else 1
-
     def sends(way, s):
         return ((k >= s) & (k < hops)) if way == 0 else ((k + s < chips) & (k > 0))
 
@@ -152,13 +149,42 @@
             def _():
                 line(g, way, s, True).wait_recv()
 
+    def busiest(way):
+        return (k == hops - 1) if way == 0 else (k == 1)
+
+    def relaxed(way, s):
+        return sends(way, s) & jnp.logical_not(busiest(way))
+
     def line_send(g, s):
         for way in (0, 1):
-            @pl.when(sends(way, s))
+            @pl.when(busiest(way))
             def _():
-                if g >= ahead(s):
-                    line(g - ahead(s), way, s, False).wait_send()
-                line(g, way, s, False).start()
+                if g >= 0:
+                    before = g * hops + s - 2
+                    if before >= 0:
+                        line(before // hops, way, before % hops, False).wait_send()
+                    line(g, way, s, False).start()
+
+            @pl.when(relaxed(way, s))
+            def _():
+                own, lag = (g + 1, 2) if s == 0 else (g, 1)
+                if own < chunks:
+                    if own >= lag:
+                        line(own - lag, way, s, False).wait_send()
+                    line(own, way, s, False).start()
+
+    def line_finish():
+        for way in (0, 1):
+            @pl.when(busiest(way))
+            def _():
+                for unit in range(max(chunks * hops - 2, 0), chunks * hops):
+                    line(unit // hops, way, unit % hops, False).wait_send()
+
+            for s in range(hops):
+                @pl.when(relaxed(way, s))
+                def _():
+                    for g in range(max(chunks - (2 if s == 0 else 1), 0), chunks):
+                        line(g, way, s, False).wait_send()
 
     square = obs_size == 4 and arcs == 2
     first = lax.rem(o, 2)
@@ -258,50 +284,45 @@
         across(g).start()
         sent.append(across(g))
 
-    def first_send(g):
+    def ready(g):
         place(g).wait()
         across_in(g).wait_recv()
+
+    own_send(0)
+    ready(0)
+    line_send(-1, 0)
+    done = 0
+    for g in range(chunks):
+        if g + 1 < chunks:
+            ready(g + 1)
         line_send(g, 0)
-
-    own_send(0)
-    for g in range(min(2, chunks)):
-        first_send(g)
-    build_filters(taps_ref, limit_ref, filt_ref)
-
-    done = 0
-    for stage in range(1, chunks + hops):
+        if g == 0:
+            build_filters(taps_ref, limit_ref, filt_ref)
         for s in range(1, hops):
-            g = stage - s
-            if 0 <= g < chunks:
-                line_wait(g, s - 1)
-                line_send(g, s)
-        if stage + 1 < chunks:
-            first_send(stage + 1)
-        if stage == 1:
+            line_wait(g, s - 1)
+            line_send(g, s)
+            if g == 0 and s == 1:
+                own_send(1)
+        if g == 0 and hops < 2:
             own_send(1)
-        g = stage - hops
-        if 0 <= g < chunks:
-            line_wait(g, hops - 1)
-            if g == 0:
-                own_forward()
-            for d in range(1, obs_size):
-                for j in range(blocks_per):
-                    block = order_ref[obs_peer(d) * blocks_per + j]
-                    stage_ref[g, d - 1, :, :, j * width : (j + 1) * width] = pools[g][block]
-                swap(g, d, o).start()
-                sent.append(swap(g, d, o))
+        line_wait(g, hops - 1)
+        if g == min(1, chunks - 1):
+            own_forward()
+        for d in range(1, obs_size):
             for j in range(blocks_per):
-                block = order_ref[o * blocks_per + j]
-                mixed_ref[g, :, epochs_of(o), j * width : (j + 1) * width] = pools[g][block]
-
-        left = chunks + hops - 1 - stage
-        if left < 3:
-            if left == 2:
-                own_wait()
-            else:
-                filter_chunk(done)
-                done += 1
-            filter_own(chunks * (2 - left) // 3, chunks * (3 - left) // 3)
+                block = order_ref[obs_peer(d) * blocks_per + j]
+                stage_ref[g, d - 1, :, :, j * width : (j + 1) * width] = pools[g][block]
+            swap(g, d, o).start()
+            sent.append(swap(g, d, o))
+        for j in range(blocks_per):
+            block = order_ref[o * blocks_per + j]
+            mixed_ref[g, :, epochs_of(o), j * width : (j + 1) * width] = pools[g][block]
+        if g == max(chunks - 2, 0):
+            own_wait()
+            filter_own(0, chunks)
+            if chunks > 1:
+                filter_chunk(0)
+                done = 1
 
     made = 0
     for g in range(done, chunks):
@@ -315,12 +336,7 @@
         back(g, 1 - core).wait_recv()
     for copy in sent:
         copy.wait_send()
-    for s in range(hops):
-        for g in range(max(chunks - ahead(s), 0), chunks):
-            for way in (0, 1):
-                @pl.when(sends(way, s))
-                def _():
-                    line(g, way, s, False).wait_send()
+    line_finish()
 
 
 def product_kernel(early, own_ref, part_ref, early_ref, out_ref, late_ref, early_s, late_s):

time: 83.8 us -> 87.8 us (1.048)
  Pallas kernels: 83.7 us -> 87.7 us
    pallas_call x1, Pallas kernels: 76.9 us -> 80.9 us  [per_device(): pl.pallas_call(functools.partial(gather_kernel, obs_size, par_size, width...]
where the time goes in v1:
time: 87.8 us; the launch traced here: 87.7 us
  Pallas kernels  87.7 us (100%)
    pallas_call x1, Pallas kernels, per_device(): pl.pallas_call(functools.partial(gather_kernel, obs_size, par_size, width...  80.9 us
    pallas_call x1, Pallas kernels, per_device(): pl.pallas_call(functools.partial(product_kernel, early), out_shape=jax.Sh...  6.74 us

profile of v1, /device:TPU:0, one launch (start us, length us, event | category | flops | bytes accessed | tf_op | source)
XLA Modules:
  0.0 87.7 jit_solution(16736191077946889132)
XLA Ops:
  0.0 80.9 %shard_map.46 = (bf16[1536,1024]{1,0:T(8,128)(2,1)S(1)}, bf16[6,2,1024,256]{3,2,1,0:T(8,128)(2,1)S(1)}, f32[2,1536,768]{2,1,0:T(8,128)S(1)}) custom-call(bf16[256,1536]{1,0:T(8,128)(2,1)} %design_ref.1, f32[2,512]{1,0:T(2,128)} %taps_ref.1, s32[2]{0:T(128)} %limit_ref.1, s32[8]{0:T(128)} %order_ref.1), custom_call_target="tpu_custom_call" | custom-call | tf_op jit(solution)/shard_map/pallas_call | solution.py:396
  80.9 6.7 %shard_map.47 = f32[1536,3072]{1,0:T(8,128)} custom-call(bf16[1536,1024]{1,0:T(8,128)(2,1)S(1)} %get-tuple-element.8.own_ref, bf16[6,2,1024,256]{3,2,1,0:T(8,128)(2,1)S(1)} %get-tuple-element.9.part_ref, f32[2,1536,768]{2,1,0:T(8,128)S(1)} %get-tuple-element.10.early_ref), custom_call_target="tpu_custom_call" | custom-call | tf_op jit(solution)/shard_map/pallas_call | solution.py:421
